TPU v7x, 256 devices: a whole 4x4x8 slice. The times are simulated.
256 devices in a mesh: orb: 64 (over y, z, core), rep: 4 (over x).
Axes of the slice: x: 4, y: 4, z: 8, core: 2. Of those that a mesh axis runs over, the one named last changes fastest.
Arguments:
- amplitudes: bfloat16 [4, 2816, 65536], P('rep', 'orb'), may hold values from -6 to 6
- integral_slab: bfloat16 [4, 2816, 8192], P('rep', None, 'orb'), may hold values from -0.0546875 to 0.0546875
- allowed_slots: int32 [8, 11264], P(None, 'rep'), may hold values 0 or 1
- row_energy: float32 [65536], P('orb'), may hold values from 0.5 to 3
- col_energy: float32 [8, 1024], P(None, 'rep'), may hold values from 0.5 to 3
Outputs:
- update: float32 [1024, 65536], P('rep', 'orb')
All inputs are finite; a program needn't handle non-finite values. No bound on the sum of `allowed_slots` on one device may be relied on, other than what follows from the above.
Results may differ from a plain program's by a relative error of at most 0.0003.
Values may be sent and summed in bfloat16 or wider, within the bound.
A program may use at most 128 MiB of HBM per device.

v0:
```python
import jax
import jax.numpy as jnp
from jax import lax
from jax.sharding import PartitionSpec as P

IRREPS = 8


def partner_2(value, axis, bit):
    mask = 2**bit
    pairs = [(source, source ^ mask) for source in range(lax.axis_size(axis))]
    return lax.ppermute(value, axis, pairs)


def doubling(own_cols, member, bit_order, partner_of):
    slot_rows = own_cols.shape[0]
    col_width = own_cols.shape[1]
    assembled = own_cols[:, None, :]
    for bit_index in bit_order:
        partner = partner_of(assembled, bit_index)
        upper_half = member // (1 << bit_index) % 2 == 1
        lower_part = jnp.where(upper_half, partner, assembled)
        upper_part = jnp.where(upper_half, assembled, partner)
        assembled = jnp.concatenate([lower_part, upper_part], axis=1)
    return assembled.reshape((slot_rows, assembled.shape[1] * col_width))


def per_device(amplitudes, integral_slab, allowed_slots, row_energy, col_energy):
    group_size = lax.axis_size("orb") // IRREPS
    orb_place = lax.axis_index("orb")
    irrep_index = orb_place // group_size
    member = orb_place % group_size
    regrouped = lax.all_to_all(amplitudes, "orb", split_axis=2, concat_axis=1, tiled=True)[0]
    allowed_row = lax.dynamic_slice_in_dim(allowed_slots, irrep_index, 1, 0)[0]
    own_cols = integral_slab[0] * allowed_row.astype(jnp.bfloat16)[:, None]
    levels = group_size.bit_length() - 1
    assembled = doubling(
        own_cols,
        member,
        list(range(levels)),
        lambda block, bit_index: partner_2(block, "orb", bit_index),
    )
    cycle_term = lax.psum_scatter(
        jnp.einsum("kc,kn->cn", assembled, regrouped, preferred_element_type=jnp.float32),
        "rep",
        scatter_dimension=0,
        tiled=True,
    )
    col_row = lax.dynamic_slice_in_dim(col_energy, irrep_index, 1, 0)[0]
    return cycle_term / (col_row[:, None] + row_energy[None, :])


def solution(mesh):
    placed = (
        P("rep", "orb", None),
        P("rep", None, "orb"),
        P(None, "rep"),
        P("orb"),
        P(None, "rep"),
    )
    return jax.shard_map(
        per_device, mesh=mesh, in_specs=placed, out_specs=P("rep", "orb"), check_vma=False
    )
```

profile of v0, /device:TPU:1, one launch (start us, length us, event | category | flops | bytes accessed | tf_op | source)
XLA Modules:
  0.0 995.0 jit_solution(11531961549232308340)
XLA Ops:
  6.5 0.0 copy-start
  6.5 62.6 %copy.12 = bf16[1,44,65536]{1,0,2:T(2,128)(2,1)} copy(bf16[1,44,65536]{2,1,0:T(8,128)(2,1)} %param.5) | data formatting | bytes 11534336 | tf_op args[0]
  69.1 0.5 broadcast.26
  69.7 355.8 %reduce.2 = bf16[65536,44]{1,0:T(8,128)(2,1)} reduce(bf16[65536,1,44]{2,1,0:T(2,128)(2,1)} %bitcast.18, bf16[]{:T(256)} %broadcast.26), dimensions={1}, to_apply=%bitcast.12.reduce_sub_computation | reduce | bytes 11534338
  425.5 47.0 %reshape.42 = bf16[64,2,22528]{2,1,0:T(2,128)(2,1)} reshape(bf16[65536,44]{1,0:T(8,128)(2,1)} %reduce.2) | data formatting | bytes 11534336
  472.5 0.0 copy-start.3
  472.5 13.6 %all-to-all-start = ((bf16[64,2,22528]{2,1,0:T(2,128)(2,1)}), bf16[64,2,22528]{2,1,0:T(2,128)(2,1)}, u32[]{:S(2)}, u32[]{:S(2)}) async-start(bf16[64,2,22528]{2,1,0:T(2,128)(2,1)} %reshape.42), calls=%async_computation | async-start | bytes 11534336 | tf_op jit(solution)/shard_map/all_to_all | solution.py:33
  486.1 0.0 reduce-scatter.2.cloned.1.call-start
  486.2 0.0 copy-done.3
  486.2 0.3 copy.11
  486.5 0.9 convert_reduce_fusion
  487.4 0.1 bitcast_multiply_fusion
  487.5 0.6 collective-permute-start
  488.1 1.8 collective-permute-done
  489.9 0.1 broadcast_select_fusion.5
  490.0 0.0 copy-start.1
  490.0 0.0 copy-start.2
  490.1 0.8 copy-done.1
  490.9 0.1 pad_maximum_fusion.2
  491.0 0.1 copy-done.2
  491.1 1.2 collective-permute-start.1
  492.4 150.6 %collective-permute-done.1 = bf16[2816,2,128]{0,2,1:T(8,128)(2,1)} collective-permute-done((bf16[2816,2,128]{0,2,1:T(8,128)(2,1)S(1)}, bf16[2816,2,128]{0,2,1:T(8,128)(2,1)}, u32[]{:S(2)}, u32[]{:S(2)}) %collective-permute-start.1) | collective-permute-done | bytes 1441824 | tf_op jit(solution)/shard_map/ppermute | solution.py:12
  643.0 1.9 broadcast_select_fusion.3
  644.9 1.9 pad_maximum_fusion.1
  646.8 1.7 collective-permute-start.2
  648.5 125.2 %collective-permute-done.2 = bf16[2816,4,128]{0,2,1:T(8,128)(2,1)} collective-permute-done((bf16[2816,4,128]{0,2,1:T(8,128)(2,1)}, bf16[2816,4,128]{0,2,1:T(8,128)(2,1)}, u32[]{:S(2)}, u32[]{:S(2)}) %collective-permute-start.2) | collective-permute-done | bytes 2883616 | tf_op jit(solution)/shard_map/ppermute | solution.py:12
  773.7 2.2 broadcast_select_fusion.1
  775.9 2.9 pad_maximum_fusion
  778.8 0.0 all-to-all-done
  778.8 59.5 %reshape.43 = bf16[65536,1,44]{2,1,0:T(2,128)(2,1)} reshape(bf16[64,2,22528]{2,1,0:T(2,128)(2,1)} %all-to-all-done) | data formatting | bytes 11534336
  838.3 63.7 %copy.13 = bf16[1,44,65536]{2,1,0:T(8,128)(2,1)} copy(bf16[1,44,65536]{1,0,2:T(2,128)(2,1)} %bitcast.19) | data formatting | bytes 11534336 | tf_op jit(solution)/shard_map/all_to_all | solution.py:33
  902.0 6.5 copy.15
  908.5 1.1 bitcast_bitcast_fusion
  909.6 5.9 copy.14
  915.5 9.1 squeeze.8
  924.6 11.1 %fusion = f32[1024,1024]{1,0:T(8,128)} fusion(bf16[2816,1024]{0,1:T(8,128)(2,1)} %bitcast.22, bf16[2816,1024]{1,0:T(8,128)(2,1)} %squeeze.8), kind=kOutput, calls=%fused_computation.14 | convolution fusion | flops 5905580032 | bytes 15728640 | tf_op jit(solution)/shard_map/kc,kn->cn/dot_general | solution.py:44
  935.8 0.0 copy-start.4
  935.8 0.0 reduce-scatter.2.cloned.1.call-update
  935.8 0.0 copy-done
  935.8 49.9 %reduce-scatter.2.cloned.1.call-done = f32[256,1024]{1,0:T(8,128)} async-done(((f32[1024,1024]{1,0:T(8,128)}), f32[256,1024]{1,0:T(8,128)}) %reduce-scatter.2.cloned.1.call-update) | async-done | bytes 1048592 | tf_op jit(solution)/shard_map/reduce_scatter | solution.py:43
  985.7 0.0 copy-done.4
  985.7 2.4 add_divide_fusion
  (1 shorter events, 0.0 us)
Async XLA Ops:
  6.5 929.3 %copy-start = (f32[8,256]{1,0:T(8,128)S(1)}, f32[8,256]{1,0:T(8,128)}, u32[]{:S(2)}) copy-start(f32[8,256]{1,0:T(8,128)} %param.9) | copy-start | bytes 24580
  472.5 13.7 %copy-start.3 = (bf16[1,2816,128]{2,1,0:T(8,128)(2,1)S(1)}, bf16[1,2816,128]{2,1,0:T(8,128)(2,1)}, u32[]{:S(2)}) copy-start(bf16[1,2816,128]{2,1,0:T(8,128)(2,1)} %param.6) | copy-start | bytes 2162692
  472.5 306.3 %all-to-all-start = ((bf16[64,2,22528]{2,1,0:T(2,128)(2,1)}), bf16[64,2,22528]{2,1,0:T(2,128)(2,1)}, u32[]{:S(2)}, u32[]{:S(2)}) async-start(bf16[64,2,22528]{2,1,0:T(2,128)(2,1)} %reshape.42), calls=%async_computation | async-start | bytes 11534336 | tf_op jit(solution)/shard_map/all_to_all | solution.py:33
  486.1 499.6 %reduce-scatter.2.cloned.1.call-start = ((), (), s32[]{:S(2)}) async-start(), calls=%async_computation.2 | async-start | bytes 5242880 | tf_op jit(solution)/shard_map/reduce_scatter | solution.py:43
  487.5 2.4 collective-permute-start
  490.0 0.9 copy-start.1
  490.0 1.1 copy-start.2
  491.1 151.9 %collective-permute-start.1 = (bf16[2816,2,128]{0,2,1:T(8,128)(2,1)S(1)}, bf16[2816,2,128]{0,2,1:T(8,128)(2,1)}, u32[]{:S(2)}, u32[]{:S(2)}) collective-permute-start(bf16[2816,2,128]{0,2,1:T(8,128)(2,1)S(1)} %pad_maximum_fusion.2), channel_id=1, source_target_pairs={{0,8},{4,12},{8,0},{12,4},{16,24},{20,28},{24,16},{28,20},{32,40},... | collective-permute-start | bytes 4325384 | tf_op jit(solution)/shard_map/ppermute | solution.py:12
  646.8 126.9 %collective-permute-start.2 = (bf16[2816,4,128]{0,2,1:T(8,128)(2,1)}, bf16[2816,4,128]{0,2,1:T(8,128)(2,1)}, u32[]{:S(2)}, u32[]{:S(2)}) collective-permute-start(bf16[2816,4,128]{0,2,1:T(8,128)(2,1)} %pad_maximum_fusion.1), channel_id=1, source_target_pairs={{0,16},{4,20},{8,24},{12,28},{16,0},{20,4},{24,8},{28,12},{32,48},... | collective-permute-start | bytes 8650760 | tf_op jit(solution)/shard_map/ppermute | solution.py:12
  935.8 50.0 %copy-start.4 = (f32[1024]{0:T(1024)S(1)}, f32[1024]{0:T(1024)}, u32[]{:S(2)}) copy-start(f32[1024]{0:T(1024)} %param.8) | copy-start | bytes 12292
Sparse Core Ops, SparseCore 0:
  935.9 49.7 reduce-scatter.1
where the time goes:
time: 1000 us; the launch traced here: 995 us
  other arithmetic  368 us (37%)
  waiting for transfers between devices  328 us (33%)
  local copies, waits for them, and re-layouts  257 us (26%)
  starting transfers between devices  17.2 us (2%)
  between operations  13.5 us (1%)
  matrix products  11.1 us (1%)
    unnamed x1, other arithmetic  356 us
    ppermute x3, waiting for transfers between devices, partner_2(): return lax.ppermute(value, axis, pairs)  278 us
    unnamed x16, local copies, waits for them, and re-layouts  177 us
    all_to_all x3, local copies, waits for them, and re-layouts, per_device(): lax.all_to_all(amplitudes, 'orb', split_axis=2, concat_axis=1, tiled=True)  70.7 us
    reduce_scatter x1, waiting for transfers between devices, per_device(): lax.psum_scatter(jnp.einsum('kc,kn->cn', assembled, regrouped, preferred_...  49.9 us
  transfers between devices with their start and end apart: 5, of which 4 were waited for; matrix products, arithmetic and copies ran while one was open for 1% of the time, Pallas kernels for 0%

commit v1 on v0

v1 whole, which is shorter than its diff:
```python
import jax
import jax.numpy as jnp
from jax import lax
from jax.experimental import pallas as pl
from jax.experimental.pallas import tpu as pltpu
from jax.sharding import PartitionSpec as P

IRREPS = 8
MESH = pl.DeviceIdType.MESH

Y, Z, CORES = 4, 8, 2
ORB = Y * Z * CORES
REP = 4
LINE = 4
SLOTS_OWN = 44
PACK = 16
CHUNKS = 4
WIDE = 256
BLOCK = CHUNKS * WIDE
COLS_OWN = 128
DEEP = 3 * ORB * PACK


def transfer(src, dst, send_sem, recv_sem, orb, rep):
    return pltpu.make_async_remote_copy(
        src_ref=src,
        dst_ref=dst,
        send_sem=send_sem,
        recv_sem=recv_sem,
        device_id=(orb, rep),
        device_id_type=MESH,
    )


def settle(ref, sem):
    pltpu.make_async_copy(ref, ref, sem).wait()


def kernel(
    amp, slab_own, row_energy, col_energy, out,
    packed, arrived, slab, part, summed,
    amp_send, amp_recv, line_send, line_recv, pair_send, pair_recv, rep_send, rep_recv,
):
    me = lax.axis_index("orb")
    rep = lax.axis_index("rep")
    y, z, core = me // (Z * CORES), (me // CORES) % Z, me % CORES
    low = z % LINE
    sibling = me + 1 - 2 * core

    def target(turn):
        i, s = turn % 8, turn // 16
        odd, half = i % 2, i // 2
        dz = (1 - odd) * (half + 1) + odd * (7 - half) - 4 * (i // 7)
        dy = (s + i + 2) % Y
        dc = 1 - (turn // 8) % 2
        return (y + dy) % Y * (Z * CORES) + (z + dz) % Z * CORES + (core + dc) % CORES

    barrier = pltpu.get_barrier_semaphore()

    @pl.loop(0, ORB - 1)
    def _(turn):
        pl.semaphore_signal(barrier, inc=1, device_id=(target(turn), rep), device_id_type=MESH)

    for step in range(1, REP):
        pl.semaphore_signal(
            barrier, inc=1, device_id=(me, (rep + step) % REP), device_id_type=MESH
        )
    pl.semaphore_wait(barrier, ORB - 1 + REP - 1)

    def to_sibling(origin):
        at = origin * CORES + core
        return transfer(
            slab.at[at], slab.at[at], pair_send.at[origin], pair_recv.at[origin], sibling, rep
        )

    def up(step):
        at = jnp.maximum(low - step, 0) * CORES + core
        return transfer(
            slab.at[at], slab.at[at], line_send.at[0, step], line_recv.at[0, step],
            (me + CORES) % ORB, rep,
        )

    def down(step):
        at = jnp.minimum(low + step, LINE - 1) * CORES + core
        return transfer(
            slab.at[at], slab.at[at], line_send.at[1, step], line_recv.at[1, step],
            (me - CORES + ORB) % ORB, rep,
        )

    def send_line(step):
        @pl.when((low < LINE - 1) & (low >= step))
        def _():
            up(step).start()

        @pl.when((low > 0) & (low <= LINE - 1 - step))
        def _():
            down(step).start()

    def receive_line(step):
        @pl.when(low >= step + 1)
        def _():
            up(step).wait_recv()
            to_sibling(low - 1 - step).start()

        @pl.when(low <= LINE - 2 - step)
        def _():
            down(step).wait_recv()
            to_sibling(low + 1 + step).start()

    own = low * CORES + core
    slab[own] = slab_own[...]
    send_line(0)
    to_sibling(low).start()

    def pack(device, ref, at):
        first = pl.multiple_of(device * BLOCK, BLOCK)
        last = amp[0, 32:SLOTS_OWN, pl.ds(first + 3 * WIDE, WIDE)].astype(jnp.float32)
        for chunk in range(CHUNKS):
            columns = pl.ds(first + chunk * WIDE, WIDE)
            ref[chunk, at, :, 0:WIDE] = amp[0, 0:16, columns]
            ref[chunk, at, :, WIDE:2 * WIDE] = amp[0, 16:32, columns]
            if chunk < CHUNKS - 1:
                rest = amp[0, 32:SLOTS_OWN, columns].astype(jnp.float32)
                tail = jnp.concatenate([rest, last[4 * chunk:4 * chunk + 4]], axis=0)
                ref[chunk, at, :, 2 * WIDE:] = tail.astype(jnp.bfloat16)

    def chunk_width(chunk):
        return 3 * WIDE if chunk < CHUNKS - 1 else 2 * WIDE

    def send_block(chunk, turn):
        columns = pl.ds(0, chunk_width(chunk))
        transfer(
            packed.at[chunk, turn, :, columns], arrived.at[chunk, me, :, columns],
            amp_send.at[chunk], amp_recv.at[chunk], target(turn), rep,
        ).start()

    def send_chunk(chunk):
        @pl.loop(0, ORB - 1)
        def _(turn):
            send_block(chunk, turn)

    @pl.loop(0, ORB - 1)
    def _(turn):
        pack(target(turn), packed, turn)
        send_block(0, turn)

    pack(me, arrived, me)
    receive_line(0)
    send_line(1)
    send_chunk(1)
    receive_line(1)
    send_line(2)
    send_chunk(2)
    receive_line(2)
    send_chunk(3)

    for origin in range(LINE):
        settle(slab.at[origin], pair_recv.at[origin])

    def contract(chunk):
        @pl.loop(0, REP)
        def _(step):
            block = (rep + 1 + step) % REP
            total = jnp.zeros((WIDE, WIDE), jnp.float32)
            for third in range(3):
                rows = slab[pl.ds(block * 2, 2), :, third * 1024:(third + 1) * 1024]
                held = arrived[chunk, :, :, third * WIDE:(third + 1) * WIDE]
                total += jnp.dot(
                    rows.reshape(2 * COLS_OWN, 1024),
                    held.reshape(1024, WIDE),
                    preferred_element_type=jnp.float32,
                )
            part[chunk, step] = total

            @pl.when(step < REP - 1)
            def _():
                transfer(
                    part.at[chunk, step], summed.at[chunk, step],
                    rep_send.at[chunk], rep_recv.at[chunk], me, block,
                ).start()

    def finish(chunk):
        settle(summed.at[chunk], rep_recv.at[chunk])
        columns = slice(chunk * WIDE, (chunk + 1) * WIDE)
        total = part[chunk, REP - 1] + summed[chunk, 0] + summed[chunk, 1] + summed[chunk, 2]
        out[:, columns] = total / (col_energy[...] + row_energy[:, columns])

    def receive_chunk(chunk):
        settle(
            arrived.at[chunk, pl.ds(0, ORB - 1), :, pl.ds(0, chunk_width(chunk))],
            amp_recv.at[chunk],
        )

    for chunk in range(CHUNKS - 1):
        receive_chunk(chunk)
        contract(chunk)
        if chunk > 0:
            finish(chunk - 1)

    low_rows = lax.broadcasted_iota(jnp.int32, (ORB * PACK, WIDE), 0) % PACK
    tails = [
        arrived[chunk, :, :, 2 * WIDE:].reshape(ORB * PACK, WIDE).astype(jnp.float32)
        for chunk in range(3)
    ]
    tail = jnp.where(
        low_rows < 4,
        pltpu.roll(tails[0], ORB * PACK - 12, 0),
        jnp.where(
            low_rows < 8,
            pltpu.roll(tails[1], ORB * PACK - 8, 0),
            pltpu.roll(tails[2], ORB * PACK - 4, 0),
        ),
    )
    arrived[CHUNKS - 1, :, :, 2 * WIDE:] = tail.astype(jnp.bfloat16).reshape(ORB, PACK, WIDE)
    finish(CHUNKS - 2)
    receive_chunk(CHUNKS - 1)
    contract(CHUNKS - 1)
    finish(CHUNKS - 1)

    for chunk in range(CHUNKS):
        settle(
            packed.at[chunk, pl.ds(0, ORB - 1), :, pl.ds(0, chunk_width(chunk))],
            amp_send.at[chunk],
        )
        settle(part.at[chunk, pl.ds(0, REP - 1)], rep_send.at[chunk])
    for step in range(LINE - 1):

        @pl.when((low < LINE - 1) & (low >= step))
        def _():
            up(step).wait_send()

        @pl.when((low > 0) & (low <= LINE - 1 - step))
        def _():
            down(step).wait_send()

    for origin in range(LINE):
        to_sibling(origin).wait_send()


def exchange(amplitudes, slab_own, row_energy, col_energy):
    vmem = pl.BlockSpec(memory_space=pltpu.VMEM)
    return pl.pallas_call(
        kernel,
        out_shape=jax.ShapeDtypeStruct((COLS_OWN * 2, BLOCK), jnp.float32),
        in_specs=[vmem] * 4,
        out_specs=vmem,
        scratch_shapes=[
            pltpu.VMEM((CHUNKS, ORB, PACK, 3 * WIDE), jnp.bfloat16),
            pltpu.VMEM((CHUNKS, ORB, PACK, 3 * WIDE), jnp.bfloat16),
            pltpu.VMEM((LINE * CORES, COLS_OWN, DEEP), jnp.bfloat16),
            pltpu.VMEM((CHUNKS, REP, WIDE, WIDE), jnp.float32),
            pltpu.VMEM((CHUNKS, REP - 1, WIDE, WIDE), jnp.float32),
            pltpu.SemaphoreType.DMA((CHUNKS,)),
            pltpu.SemaphoreType.DMA((CHUNKS,)),
            pltpu.SemaphoreType.DMA((2, LINE - 1)),
            pltpu.SemaphoreType.DMA((2, LINE - 1)),
            pltpu.SemaphoreType.DMA((LINE,)),
            pltpu.SemaphoreType.DMA((LINE,)),
            pltpu.SemaphoreType.DMA((CHUNKS,)),
            pltpu.SemaphoreType.DMA((CHUNKS,)),
        ],
        compiler_params=pltpu.CompilerParams(
            collective_id=0, has_side_effects=True, vmem_limit_bytes=56 * 2**20
        ),
        cost_estimate=pl.CostEstimate(
            flops=2 * 1024 * BLOCK * DEEP, bytes_accessed=8 * 2**20, transcendentals=0
        ),
    )(amplitudes, slab_own, row_energy, col_energy)


def per_device(amplitudes, integral_slab, allowed_slots, row_energy, col_energy):
    irrep_index = lax.axis_index("orb") // (lax.axis_size("orb") // IRREPS)
    allowed_row = lax.dynamic_slice_in_dim(allowed_slots, irrep_index, 1, 0)[0]
    live = integral_slab[0] * allowed_row.astype(jnp.bfloat16)[:, None]
    live = jnp.pad(live.reshape(ORB, SLOTS_OWN, COLS_OWN), ((0, 0), (0, 48 - SLOTS_OWN), (0, 0)))
    live = live.reshape(ORB, 3, PACK, COLS_OWN).transpose(3, 1, 0, 2).reshape(COLS_OWN, DEEP)
    col_row = lax.dynamic_slice_in_dim(col_energy, irrep_index, 1, 0)[0]
    return exchange(amplitudes, live, row_energy[None, :], col_row[:, None])


def solution(mesh):
    placed = (
        P("rep", "orb", None),
        P("rep", None, "orb"),
        P(None, "rep"),
        P("orb"),
        P(None, "rep"),
    )
    return jax.shard_map(
        per_device, mesh=mesh, in_specs=placed, out_specs=P("rep", "orb"), check_vma=False
    )
```

time: 1000 us -> 227 us (0.23)
  other arithmetic: 368 us -> 1.4 us
  waiting for transfers between devices: 328 us -> 0 us
  local copies, waits for them, and re-layouts: 257 us -> 6.54 us
  Pallas kernels: 0 us -> 219 us
  starting transfers between devices: 17.2 us -> 0 us
  between operations: 13.5 us -> 0.04 us
  matrix products: 11.1 us -> 0 us
    unnamed x1 -> x0, other arithmetic: 356 us -> none
    ppermute x3 -> x0, waiting for transfers between devices: 278 us -> none  [partner_2(): return lax.ppermute(value, axis, pairs)]
    pallas_call x0 -> x1, Pallas kernels: none -> 219 us  [exchange(): pl.pallas_call(kernel, out_shape=jax.ShapeDtypeStruct((COLS_OWN * 2, BLOC...]
    unnamed x16 -> x3, local copies, waits for them, and re-layouts: 177 us -> 3 us
    all_to_all x3 -> x0, local copies, waits for them, and re-layouts: 70.7 us -> none  [per_device(): lax.all_to_all(amplitudes, 'orb', split_axis=2, concat_axis=1, tiled=True)]
    reduce_scatter x1 -> x0, waiting for transfers between devices: 49.9 us -> none  [per_device(): lax.psum_scatter(jnp.einsum('kc,kn->cn', assembled, regrouped, preferred_...]
    all_to_all x1 -> x0, starting transfers between devices: 13.6 us -> none  [per_device(): lax.all_to_all(amplitudes, 'orb', split_axis=2, concat_axis=1, tiled=True)]
    dot_general x1 -> x0, matrix products: 11.1 us -> none  [per_device(): jnp.einsum('kc,kn->cn', assembled, regrouped, preferred_element_type=jnp....]
  transfers between devices with their start and end apart: 5 -> 0, of which waited for: 4 -> 0; matrix products, arithmetic and copies ran while one was open for 1% -> 0% of each run, Pallas kernels for 0% -> 0%
where the time goes in v1:
time: 227 us
  Pallas kernels  219 us (96%)
  local copies, waits for them, and re-layouts  6.54 us (3%)
    pallas_call x1, Pallas kernels, exchange(): pl.pallas_call(kernel, out_shape=jax.ShapeDtypeStruct((COLS_OWN * 2, BLOC...  219 us

profile of v1, /device:TPU:1, one launch (start us, length us, event | category | flops | bytes accessed | tf_op | source)
XLA Modules:
  0.0 226.6 jit_solution(2702004031838489181)
XLA Ops:
  0.0 0.0 copy-start
  0.0 0.7 copy-done
  0.7 0.9 convert_reduce_fusion
  1.6 0.1 convert_element_type.13
  1.8 0.8 copy.8.col_energy
  2.6 1.2 squeeze.4
  3.8 0.5 broadcast_multiply_fusion
  4.3 0.1 pad.4
  4.3 0.1 copy.6
  4.5 1.2 copy.7.slab_own
  5.7 218.6 %shard_map.55 = f32[256,1024]{1,0:T(8,128)} custom-call(bf16[1,44,65536]{2,1,0:T(8,128)(2,1)} %amp.1, bf16[128,3072]{1,0:T(8,128)(2,1)} %copy.7.slab_own, f32[1,1024]{1,0:T(1,128)} %bitcast.9, f32[256,1]{1,0:T(8,128)} %copy.8.col_energy), custom_call_target="tpu_custom_call" | custom-call | flops 6442450944 | bytes 8388608 | tf_op jit(solution)/shard_map/pallas_call | solution.py:242
  224.3 2.3 %copy.10 = f32[256,1024]{1,0:T(8,128)} copy(f32[256,1024]{1,0:T(8,128)} %shard_map.55) | data formatting | bytes 2097152
  (1 shorter events, 0.0 us)
Async XLA Ops:
  0.0 0.7 copy-start

commit v2 on v0

v2 whole, which is shorter than its diff:
```python
import jax
import jax.numpy as jnp
from jax import lax
from jax.experimental import pallas as pl
from jax.experimental.pallas import tpu as pltpu
from jax.sharding import PartitionSpec as P

IRREPS = 8
MESH = pl.DeviceIdType.MESH

Y, Z, CORES = 4, 8, 2
ORB = Y * Z * CORES
REP = 4
LINE = 4
QUARTERS = 4
SOURCES = ORB // QUARTERS
TARGETS = ORB // 2
SLOTS_OWN = 44
PACK = 16
THIRDS = 3
CHUNKS = 8
FULL = 6
NARROW = 128
WIDE = 2 * NARROW
BLOCK = CHUNKS * NARROW
COLS_OWN = 128
COLS_OUT = 256
QUARTER = THIRDS * SOURCES * PACK
DEEP = 2 * QUARTER
ROWS_Y = Z * CORES * SLOTS_OWN
COLUMNS = Z * CORES * THIRDS * PACK
PIECES = [(chunk, pl.ds(0, WIDE)) for chunk in range(CHUNKS - 1)]
PIECES += [(CHUNKS - 1, pl.ds(0, NARROW)), (CHUNKS - 1, pl.ds(NARROW, NARROW))]


def transfer(src, dst, send_sem, recv_sem, orb, rep):
    return pltpu.make_async_remote_copy(
        src_ref=src,
        dst_ref=dst,
        send_sem=send_sem,
        recv_sem=recv_sem,
        device_id=(orb, rep),
        device_id_type=MESH,
    )


def settle(ref, sem):
    pltpu.make_async_copy(ref, ref, sem).wait()


def kernel(
    amp, integrals, allowed, row_energy, col_energy, out,
    stage, packed, arrived, order, slab_own, slab, part, summed, both, cross,
    stage_sem, amp_send, amp_recv, line_send, line_recv, pair_send, pair_recv,
    rep_send, rep_recv, cross_send, cross_recv,
):
    me = lax.axis_index("orb")
    rep = lax.axis_index("rep")
    y, z, core = me // (Z * CORES), (me // CORES) % Z, me % CORES
    low, high = z % LINE, z // LINE
    upper = low // 2
    sibling = me + 1 - 2 * core
    partner = me + 2 * CORES - 4 * CORES * upper

    def device(y, z, core):
        return y * (Z * CORES) + z * CORES + core

    def target(turn):
        kind, s = turn % 4, turn // 4
        near = kind % 2
        half = (1 - near) * (kind // 2) + near * (upper + (kind // 2) * (1 - 2 * upper))
        group = (high + 1 - near) % 2
        quarter = ((z - LINE * group + Z + 3) // 2) % QUARTERS
        place = (quarter - half + LINE) % LINE
        to_y = (y + s + kind + 2) % Y
        to_core = (core + 1 - s // 4) % CORES
        return to_y, group, place, to_core, half

    def target_id(turn):
        to_y, group, place, to_core, _ = target(turn)
        return device(to_y, group * LINE + place, to_core)

    def first_rows(turn):
        to_y, group, place, to_core, _ = target(turn)
        return device(to_y, group * LINE + place % 2, to_core)

    def load(turn, side):
        base = pl.multiple_of((first_rows(turn) + side * 2 * CORES) * BLOCK, BLOCK)
        return pltpu.make_async_copy(
            amp.at[0, :, pl.ds(base, BLOCK)], stage.at[turn, side], stage_sem.at[turn, side]
        )

    @pl.loop(0, TARGETS)
    def _(turn):
        load(turn, 0).start()
        load(turn, 1).start()

    barrier = pltpu.get_barrier_semaphore()

    @pl.loop(0, TARGETS)
    def _(index):
        step = index // (Y * CORES)
        from_z = (LINE * high + 2 * low - 3 + step + Z) % Z
        source = device((index // CORES) % Y, from_z, index % CORES)

        @pl.when(source != me)
        def _():
            pl.semaphore_signal(barrier, inc=1, device_id=(source, rep), device_id_type=MESH)

    for step in range(1, REP):
        pl.semaphore_signal(
            barrier, inc=1, device_id=(me, (rep + step) % REP), device_id_type=MESH
        )
    for step in range(1, LINE):
        pl.semaphore_signal(
            barrier, inc=1,
            device_id=(me + CORES * ((low + step) % LINE - low), rep), device_id_type=MESH,
        )
    pl.semaphore_signal(barrier, inc=1, device_id=(sibling, rep), device_id_type=MESH)
    pl.semaphore_wait(barrier, TARGETS - 1 + REP - 1 + LINE - 1 + 1)

    own = low * CORES + core

    def quarter_of(place, half):
        quarter = (place + half + 2 + 2 * high) % QUARTERS
        return pl.ds(pl.multiple_of(quarter * QUARTER, QUARTER), QUARTER)

    def order_slab():
        across = lax.broadcasted_iota(jnp.int32, (1, COLUMNS), 1)
        piece, within = across // 64, across % 64
        slot = piece % THIRDS * PACK + within % PACK
        from_z = (2 * (piece // THIRDS) + 1 + within // 32) % Z
        row = (from_z * CORES + within // PACK % CORES) * SLOTS_OWN + slot
        row = jnp.where(slot < SLOTS_OWN, row, -1)
        down = lax.broadcasted_iota(jnp.int32, (ROWS_Y, COLUMNS), 0)
        order[...] = jnp.where(down == row, 1.0, 0.0).astype(jnp.bfloat16)
        irrep = lax.broadcasted_iota(jnp.int32, (IRREPS, COLUMNS), 0)
        for at_y in range(Y):
            rows = slice(at_y * ROWS_Y, (at_y + 1) * ROWS_Y)
            live = lax.dot_general(
                integrals[0, rows], order[...], (((0,), (0,)), ((), ())),
                preferred_element_type=jnp.float32,
            )
            mask = jnp.dot(
                allowed[:, rows].astype(jnp.float32).astype(jnp.bfloat16), order[...],
                preferred_element_type=jnp.float32,
            )
            mask = jnp.sum(
                jnp.where(irrep == me // (ORB // IRREPS), mask, 0.0), axis=0, keepdims=True
            )
            live = (live * mask).astype(jnp.bfloat16)
            for piece in range(QUARTERS * THIRDS):
                first = piece * SOURCES * PACK + at_y * 64
                slab_own[:, first:first + 64] = live[:, piece * 64:(piece + 1) * 64]

    def to_sibling(step):
        at = (low - step + LINE) % LINE * CORES + core
        return transfer(
            slab.at[at], slab.at[at], pair_send.at[step], pair_recv.at[step], sibling, rep
        )

    def send_slab(step, half):
        place = (low + step) % LINE
        transfer(
            slab_own.at[:, quarter_of(place, half)],
            slab.at[own, :, pl.ds(half * QUARTER, QUARTER)],
            line_send.at[step - 1], line_recv.at[step - 1], me + CORES * (place - low), rep,
        ).start()

    def pack(turn, store):
        for side in range(2):
            load(turn, side).wait()
            lanes = slice(side * NARROW, (side + 1) * NARROW)

            def read(first, last, chunk):
                return stage[turn, side, first:last, chunk * NARROW:(chunk + 1) * NARROW]

            lasts = [read(32, SLOTS_OWN, chunk).astype(jnp.float32) for chunk in range(FULL, CHUNKS)]
            for chunk in range(CHUNKS):
                store(chunk, 0, lanes, read(0, 16, chunk))
                store(chunk, 1, lanes, read(16, 32, chunk))
                if chunk < FULL:
                    rest = read(32, SLOTS_OWN, chunk).astype(jnp.float32)
                    at = 4 * (chunk % 3)
                    tail = jnp.concatenate([rest, lasts[chunk // 3][at:at + 4]], axis=0)
                    store(chunk, 2, lanes, tail.astype(jnp.bfloat16))

    source_at = y * (2 * CORES) + (z + 1) % 2 * CORES + core

    def thirds(chunk):
        return pl.ds(0, THIRDS if chunk < FULL else 2)

    def send_block(piece, turn):
        chunk, lanes = PIECES[piece]
        half = target(turn)[-1]
        transfer(
            packed.at[chunk, turn, thirds(chunk), :, lanes],
            arrived.at[chunk, half, thirds(chunk), source_at, :, lanes],
            amp_send.at[piece], amp_recv.at[piece], target_id(turn), rep,
        ).start()

    def send_piece(piece, first=0, last=TARGETS - 1):
        @pl.loop(first, last)
        def _(turn):
            send_block(piece, turn)

    def sent(piece):
        chunk, lanes = PIECES[piece]
        return packed.at[chunk, pl.ds(0, TARGETS - 1), thirds(chunk), :, lanes]

    @pl.loop(0, TARGETS - 1)
    def _(turn):
        def store(chunk, third, lanes, value):
            packed[chunk, turn, third, :, lanes] = value

        pack(turn, store)
        send_block(0, turn)

    def store_own(chunk, third, lanes, value):
        arrived[chunk, 1 - upper, third, source_at, :, lanes] = value

    pack(TARGETS - 1, store_own)
    order_slab()
    for part_of in range(6):
        send_slab(1 + part_of % 3, part_of // 3)
        send_piece(1, part_of * 5, part_of * 5 + 5 if part_of < 5 else TARGETS - 1)
    for half in range(2):
        slab[own, :, half * QUARTER:(half + 1) * QUARTER] = slab_own[:, quarter_of(low, half)]
    to_sibling(0).start()
    send_piece(2)
    for step in range(1, LINE):
        at = (low - step + LINE) % LINE * CORES + core
        settle(slab.at[at], line_recv.at[step - 1])
        to_sibling(step).start()
    send_piece(3)
    for step in range(LINE):
        settle(slab.at[own], pair_recv.at[step])

    def contract(piece):
        chunk, lanes = PIECES[piece]

        @pl.loop(0, REP)
        def _(step):
            block = (rep + 1 + step) % REP
            rows = slab[pl.ds(block * 2, 2)].reshape(COLS_OUT, DEEP)
            part[chunk, step, :, lanes] = jnp.dot(
                rows,
                arrived[chunk, :, :, :, :, lanes].reshape(DEEP, lanes.size),
                preferred_element_type=jnp.float32,
            )

            @pl.when(step < REP - 1)
            def _():
                transfer(
                    part.at[chunk, step, :, lanes], summed.at[chunk, step, :, lanes],
                    rep_send.at[piece], rep_recv.at[piece], me, block,
                ).start()

    own_lanes = pl.ds(pl.multiple_of(upper * NARROW, NARROW), NARROW)
    other_lanes = pl.ds(pl.multiple_of((1 - upper) * NARROW, NARROW), NARROW)

    def to_partner(chunk):
        return transfer(
            both.at[chunk, :, other_lanes], cross.at[chunk],
            cross_send.at[chunk], cross_recv.at[chunk], partner, rep,
        )

    def sum_quarters(piece):
        chunk, lanes = PIECES[piece]
        settle(summed.at[chunk, :, :, lanes], rep_recv.at[piece])
        total = part[chunk, REP - 1, :, lanes]
        for step in range(REP - 1):
            total += summed[chunk, step, :, lanes]
        both[chunk, :, lanes] = total
        if lanes.size == WIDE:
            to_partner(chunk).start()
        else:

            @pl.when(upper == 1 - lanes.start // NARROW)
            def _():
                to_partner(chunk).start()

    def finish(chunk):
        to_partner(chunk).wait_recv()
        columns = slice(chunk * NARROW, (chunk + 1) * NARROW)
        total = both[chunk, :, own_lanes] + cross[chunk]
        out[:, columns] = total / (col_energy[...] + row_energy[:, columns])

    def gather_tail(chunk):
        rows = 2 * SOURCES * PACK
        place = lax.broadcasted_iota(jnp.int32, (rows, WIDE), 0) % PACK
        first = (chunk - FULL) * 3
        tails = [
            pltpu.roll(
                arrived[first + i, :, 2].reshape(rows, WIDE).astype(jnp.float32),
                rows - 12 + 4 * i,
                0,
            )
            for i in range(3)
        ]
        tail = jnp.where(place < 4, tails[0], jnp.where(place < 8, tails[1], tails[2]))
        arrived[chunk, :, 2] = tail.astype(jnp.bfloat16).reshape(2, SOURCES, PACK, WIDE)

    for piece, (chunk, _) in enumerate(PIECES):
        settle(sent(piece), amp_recv.at[piece])
        if piece + 4 < len(PIECES):
            send_piece(piece + 4)
        contract(piece)
        if piece >= 1:
            sum_quarters(piece - 1)
        if 2 <= piece <= CHUNKS:
            finish(piece - 2)
        if piece == 2:
            gather_tail(FULL)
        if piece == 5:
            gather_tail(FULL + 1)
    sum_quarters(len(PIECES) - 1)
    finish(CHUNKS - 1)

    for piece, (chunk, lanes) in enumerate(PIECES):
        settle(sent(piece), amp_send.at[piece])
        settle(part.at[chunk, pl.ds(0, REP - 1), :, lanes], rep_send.at[piece])
    for chunk in range(CHUNKS):
        to_partner(chunk).wait_send()
    for step in range(LINE - 1):
        settle(slab.at[own], line_send.at[step])
    for step in range(LINE):
        settle(slab.at[own], pair_send.at[step])


def per_device(amplitudes, integral_slab, allowed_slots, row_energy, col_energy):
    irrep_index = lax.axis_index("orb") // (lax.axis_size("orb") // IRREPS)
    col_row = lax.dynamic_slice_in_dim(col_energy, irrep_index, 1, 0)[0]
    vmem = pl.BlockSpec(memory_space=pltpu.VMEM)
    pairs = lambda count: [pltpu.SemaphoreType.DMA((count,))] * 2
    return pl.pallas_call(
        kernel,
        out_shape=jax.ShapeDtypeStruct((COLS_OUT, BLOCK), jnp.float32),
        in_specs=[pl.BlockSpec(memory_space=pl.ANY)] + [vmem] * 4,
        out_specs=vmem,
        scratch_shapes=[
            pltpu.VMEM((TARGETS, 2, SLOTS_OWN, BLOCK), jnp.bfloat16),
            pltpu.VMEM((CHUNKS, TARGETS, THIRDS, PACK, WIDE), jnp.bfloat16),
            pltpu.VMEM((CHUNKS, 2, THIRDS, SOURCES, PACK, WIDE), jnp.bfloat16),
            pltpu.VMEM((ROWS_Y, COLUMNS), jnp.bfloat16),
            pltpu.VMEM((COLS_OWN, QUARTERS * QUARTER), jnp.bfloat16),
            pltpu.VMEM((LINE * CORES, COLS_OWN, DEEP), jnp.bfloat16),
            pltpu.VMEM((CHUNKS, REP, COLS_OUT, WIDE), jnp.float32),
            pltpu.VMEM((CHUNKS, REP - 1, COLS_OUT, WIDE), jnp.float32),
            pltpu.VMEM((CHUNKS, COLS_OUT, WIDE), jnp.float32),
            pltpu.VMEM((CHUNKS, COLS_OUT, NARROW), jnp.float32),
            pltpu.SemaphoreType.DMA((TARGETS, 2)),
            *pairs(len(PIECES)),
            *pairs(LINE - 1),
            *pairs(LINE),
            *pairs(len(PIECES)),
            *pairs(CHUNKS),
        ],
        compiler_params=pltpu.CompilerParams(
            collective_id=0, has_side_effects=True, vmem_limit_bytes=56 * 2**20
        ),
        cost_estimate=pl.CostEstimate(
            flops=2 * 1024 * WIDE * CHUNKS * DEEP, bytes_accessed=8 * 2**20, transcendentals=0
        ),
    )(amplitudes, integral_slab, allowed_slots, row_energy[None, :], col_row[:, None])


def solution(mesh):
    placed = (
        P("rep", "orb", None),
        P("rep", None, "orb"),
        P(None, "rep"),
        P("orb"),
        P(None, "rep"),
    )
    return jax.shard_map(
        per_device, mesh=mesh, in_specs=placed, out_specs=P("rep", "orb"), check_vma=False
    )
```

time: 1000 us -> 179 us (0.18)
  other arithmetic: 368 us -> 0 us
  waiting for transfers between devices: 328 us -> 0 us
  local copies, waits for them, and re-layouts: 257 us -> 3.81 us
  Pallas kernels: 0 us -> 173 us
  starting transfers between devices: 17.2 us -> 0 us
  between operations: 13.5 us -> 0.01 us
  matrix products: 11.1 us -> 0 us
    unnamed x1 -> x0, other arithmetic: 356 us -> none
    ppermute x3 -> x0, waiting for transfers between devices: 278 us -> none  [partner_2(): return lax.ppermute(value, axis, pairs)]
    unnamed x16 -> x3, local copies, waits for them, and re-layouts: 177 us -> 3 us
    pallas_call x0 -> x1, Pallas kernels: none -> 173 us  [per_device(): pl.pallas_call(kernel, out_shape=jax.ShapeDtypeStruct((COLS_OUT, BLOCK),...]
    all_to_all x3 -> x0, local copies, waits for them, and re-layouts: 70.7 us -> none  [per_device(): lax.all_to_all(amplitudes, 'orb', split_axis=2, concat_axis=1, tiled=True)]
    reduce_scatter x1 -> x0, waiting for transfers between devices: 49.9 us -> none  [per_device(): lax.psum_scatter(jnp.einsum('kc,kn->cn', assembled, regrouped, preferred_...]
    all_to_all x1 -> x0, starting transfers between devices: 13.6 us -> none  [per_device(): lax.all_to_all(amplitudes, 'orb', split_axis=2, concat_axis=1, tiled=True)]
    dot_general x1 -> x0, matrix products: 11.1 us -> none  [per_device(): jnp.einsum('kc,kn->cn', assembled, regrouped, preferred_element_type=jnp....]
  transfers between devices with their start and end apart: 5 -> 0, of which waited for: 4 -> 0; matrix products, arithmetic and copies ran while one was open for 1% -> 0% of each run, Pallas kernels for 0% -> 0%
where the time goes in v2:
time: 179 us; the launch traced here: 177 us
  Pallas kernels  173 us (97%)
  local copies, waits for them, and re-layouts  3.81 us (2%)
    pallas_call x1, Pallas kernels, per_device(): pl.pallas_call(kernel, out_shape=jax.ShapeDtypeStruct((COLS_OUT, BLOCK),...  173 us

profile of v2, /device:TPU:1, one launch (start us, length us, event | category | flops | bytes accessed | tf_op | source)
XLA Modules:
  0.0 177.3 jit_solution(16324572175512921568)
XLA Ops:
  0.0 0.0 copy-start
  0.0 0.7 copy-done
  0.7 0.8 copy.6.col_energy
  1.5 173.4 %shard_map.55 = f32[256,1024]{1,0:T(8,128)} custom-call(bf16[1,44,65536]{2,1,0:T(8,128)(2,1)} %amp.1, bf16[1,2816,128]{2,1,0:T(8,128)(2,1)} %integrals.1, s32[8,2816]{1,0:T(8,128)} %allowed.1, f32[1,1024]{1,0:T(1,128)} %bitcast.3, f32[256,1]{1,0:T(8,128)} %copy.6.col_energy), custom_call_target="tpu_custom_call" | custom-call | flops 6442450944 | bytes 8388608 | tf_op jit(solution)/shard_map/pallas_call | solution.py:336
  175.0 2.3 %copy.8 = f32[256,1024]{1,0:T(8,128)} copy(f32[256,1024]{1,0:T(8,128)} %shard_map.55) | data formatting | bytes 2097152
  (1 shorter events, 0.0 us)
Async XLA Ops:
  0.0 0.7 copy-start

commit v3 on v2

--- a/solution.py
+++ b/solution.py
@@ -25,6 +25,8 @@
 BLOCK = CHUNKS * NARROW
 COLS_OWN = 128
 COLS_OUT = 256
+HALF = COLS_OUT // 2
+OPPOSITE, OWN, BESIDE = 0, 2, (1, 3)
 QUARTER = THIRDS * SOURCES * PACK
 DEEP = 2 * QUARTER
 ROWS_Y = Z * CORES * SLOTS_OWN
@@ -50,9 +52,9 @@
 
 def kernel(
     amp, integrals, allowed, row_energy, col_energy, out,
-    stage, packed, arrived, order, slab_own, slab, part, summed, both, cross,
+    stage, packed, arrived, order, slab_own, slab, part, near, summed, both, cross,
     stage_sem, amp_send, amp_recv, line_send, line_recv, pair_send, pair_recv,
-    rep_send, rep_recv, cross_send, cross_recv,
+    near_recv, rep_send, rep_recv, cross_send, cross_recv,
 ):
     me = lax.axis_index("orb")
     rep = lax.axis_index("rep")
@@ -232,16 +234,38 @@
         at = (low - step + LINE) % LINE * CORES + core
         settle(slab.at[at], line_recv.at[step - 1])
         to_sibling(step).start()
-    send_piece(3)
     for step in range(LINE):
         settle(slab.at[own], pair_recv.at[step])
 
+    def to_side(piece, way, src, dst, sem):
+        return transfer(
+            src, dst, rep_send.at[piece], sem, me, (rep + 1 + 2 * way) % REP
+        )
+
+    def half_rows(way):
+        return pl.ds(way * HALF, HALF)
+
+    def through(piece, way):
+        chunk, lanes = PIECES[piece]
+        return to_side(
+            piece, way, part.at[chunk, OPPOSITE, half_rows(way), lanes],
+            near.at[chunk, way, :, lanes], near_recv.at[piece],
+        )
+
+    def direct(piece, way, half):
+        chunk, lanes = PIECES[piece]
+        rows = half_rows(half)
+        return to_side(
+            piece, way, part.at[chunk, BESIDE[way], rows, lanes],
+            summed.at[chunk, way, rows, lanes], rep_recv.at[piece],
+        )
+
     def contract(piece):
         chunk, lanes = PIECES[piece]
 
         @pl.loop(0, REP)
         def _(step):
-            block = (rep + 1 + step) % REP
+            block = (rep + 2 + 3 * step) % REP
             rows = slab[pl.ds(block * 2, 2)].reshape(COLS_OUT, DEEP)
             part[chunk, step, :, lanes] = jnp.dot(
                 rows,
@@ -249,12 +273,23 @@
                 preferred_element_type=jnp.float32,
             )
 
-            @pl.when(step < REP - 1)
+            @pl.when(step == OPPOSITE)
             def _():
-                transfer(
-                    part.at[chunk, step, :, lanes], summed.at[chunk, step, :, lanes],
-                    rep_send.at[piece], rep_recv.at[piece], me, block,
-                ).start()
+                through(piece, 0).start()
+                through(piece, 1).start()
+
+            for way in range(2):
+
+                @pl.when(step == BESIDE[way])
+                def _():
+                    direct(piece, way, 1 - way).start()
+
+    def pass_on(piece):
+        chunk, lanes = PIECES[piece]
+        settle(near.at[chunk, :, :, lanes], near_recv.at[piece])
+        for way in range(2):
+            part[chunk, BESIDE[way], half_rows(way), lanes] += near[chunk, way, :, lanes]
+            direct(piece, way, way).start()
 
     own_lanes = pl.ds(pl.multiple_of(upper * NARROW, NARROW), NARROW)
     other_lanes = pl.ds(pl.multiple_of((1 - upper) * NARROW, NARROW), NARROW)
@@ -268,10 +303,8 @@
     def sum_quarters(piece):
         chunk, lanes = PIECES[piece]
         settle(summed.at[chunk, :, :, lanes], rep_recv.at[piece])
-        total = part[chunk, REP - 1, :, lanes]
-        for step in range(REP - 1):
-            total += summed[chunk, step, :, lanes]
-        both[chunk, :, lanes] = total
+        total = part[chunk, OWN, :, lanes] + summed[chunk, 0, :, lanes]
+        both[chunk, :, lanes] = total + summed[chunk, 1, :, lanes]
         if lanes.size == WIDE:
             to_partner(chunk).start()
         else:
@@ -303,8 +336,8 @@
 
     for piece, (chunk, _) in enumerate(PIECES):
         settle(sent(piece), amp_recv.at[piece])
-        if piece + 4 < len(PIECES):
-            send_piece(piece + 4)
+        if piece + 3 < len(PIECES):
+            send_piece(piece + 3)
         contract(piece)
         if piece >= 1:
             sum_quarters(piece - 1)
@@ -314,6 +347,7 @@
             gather_tail(FULL)
         if piece == 5:
             gather_tail(FULL + 1)
+        pass_on(piece)
     sum_quarters(len(PIECES) - 1)
     finish(CHUNKS - 1)
 
@@ -346,13 +380,15 @@
             pltpu.VMEM((COLS_OWN, QUARTERS * QUARTER), jnp.bfloat16),
             pltpu.VMEM((LINE * CORES, COLS_OWN, DEEP), jnp.bfloat16),
             pltpu.VMEM((CHUNKS, REP, COLS_OUT, WIDE), jnp.float32),
-            pltpu.VMEM((CHUNKS, REP - 1, COLS_OUT, WIDE), jnp.float32),
+            pltpu.VMEM((CHUNKS, 2, HALF, WIDE), jnp.float32),
+            pltpu.VMEM((CHUNKS, 2, COLS_OUT, WIDE), jnp.float32),
             pltpu.VMEM((CHUNKS, COLS_OUT, WIDE), jnp.float32),
             pltpu.VMEM((CHUNKS, COLS_OUT, NARROW), jnp.float32),
             pltpu.SemaphoreType.DMA((TARGETS, 2)),
             *pairs(len(PIECES)),
             *pairs(LINE - 1),
             *pairs(LINE),
+            pltpu.SemaphoreType.DMA((len(PIECES),)),
             *pairs(len(PIECES)),
             *pairs(CHUNKS),
         ],

time: 179 us -> 170 us (0.950)
  Pallas kernels: 173 us -> 163 us
    pallas_call x1, Pallas kernels: 173 us -> 163 us  [per_device(): pl.pallas_call(kernel, out_shape=jax.ShapeDtypeStruct((COLS_OUT, BLOCK),...]
where the time goes in v3:
time: 170 us; the launch traced here: 167 us
  Pallas kernels  163 us (96%)
  local copies, waits for them, and re-layouts  3.81 us (2%)
    pallas_call x1, Pallas kernels, per_device(): pl.pallas_call(kernel, out_shape=jax.ShapeDtypeStruct((COLS_OUT, BLOCK),...  163 us

profile of v3, /device:TPU:1, one launch (start us, length us, event | category | flops | bytes accessed | tf_op | source)
XLA Modules:
  0.0 167.1 jit_solution(18353073650275764587)
XLA Ops:
  0.0 0.0 copy-start
  0.0 0.7 copy-done
  0.7 0.8 copy.6.col_energy
  1.5 163.3 %shard_map.55 = f32[256,1024]{1,0:T(8,128)} custom-call(bf16[1,44,65536]{2,1,0:T(8,128)(2,1)} %amp.1, bf16[1,2816,128]{2,1,0:T(8,128)(2,1)} %integrals.1, s32[8,2816]{1,0:T(8,128)} %allowed.1, f32[1,1024]{1,0:T(1,128)} %bitcast.3, f32[256,1]{1,0:T(8,128)} %copy.6.col_energy), custom_call_target="tpu_custom_call" | custom-call | flops 6442450944 | bytes 8388608 | tf_op jit(solution)/shard_map/pallas_call | solution.py:370
  164.8 2.3 %copy.8 = f32[256,1024]{1,0:T(8,128)} copy(f32[256,1024]{1,0:T(8,128)} %shard_map.55) | data formatting | bytes 2097152
  (1 shorter events, 0.0 us)
Async XLA Ops:
  0.0 0.7 copy-start

commit v4 on v3

--- a/solution.py
+++ b/solution.py
@@ -26,13 +26,14 @@
 COLS_OWN = 128
 COLS_OUT = 256
 HALF = COLS_OUT // 2
-OPPOSITE, OWN, BESIDE = 0, 2, (1, 3)
+OPPOSITE, OWN, BESIDE = 0, 3, (1, 2)
 QUARTER = THIRDS * SOURCES * PACK
 DEEP = 2 * QUARTER
 ROWS_Y = Z * CORES * SLOTS_OWN
 COLUMNS = Z * CORES * THIRDS * PACK
 PIECES = [(chunk, pl.ds(0, WIDE)) for chunk in range(CHUNKS - 1)]
 PIECES += [(CHUNKS - 1, pl.ds(0, NARROW)), (CHUNKS - 1, pl.ds(NARROW, NARROW))]
+SENT_AFTER = {piece: (piece + 3,) for piece in range(CHUNKS - 2)}
 
 
 def transfer(src, dst, send_sem, recv_sem, orb, rep):
@@ -265,7 +266,7 @@
 
         @pl.loop(0, REP)
         def _(step):
-            block = (rep + 2 + 3 * step) % REP
+            block = (rep + 2 + 3 * step + 3 * (step // 2) + 2 * (step // 3)) % REP
             rows = slab[pl.ds(block * 2, 2)].reshape(COLS_OUT, DEEP)
             part[chunk, step, :, lanes] = jnp.dot(
                 rows,
@@ -334,22 +335,28 @@
         tail = jnp.where(place < 4, tails[0], jnp.where(place < 8, tails[1], tails[2]))
         arrived[chunk, :, 2] = tail.astype(jnp.bfloat16).reshape(2, SOURCES, PACK, WIDE)
 
+    middle = TARGETS // 2
+    done = 0
     for piece, (chunk, _) in enumerate(PIECES):
         settle(sent(piece), amp_recv.at[piece])
-        if piece + 3 < len(PIECES):
-            send_piece(piece + 3)
+        for later in SENT_AFTER.get(piece, ()):
+            send_piece(later, 0, middle)
         contract(piece)
         if piece >= 1:
             sum_quarters(piece - 1)
-        if 2 <= piece <= CHUNKS:
-            finish(piece - 2)
         if piece == 2:
             gather_tail(FULL)
         if piece == 5:
             gather_tail(FULL + 1)
         pass_on(piece)
+        for later in SENT_AFTER.get(piece, ()):
+            send_piece(later, middle, TARGETS - 1)
+        while done < PIECES[piece - 1][0] and piece >= 2:
+            finish(done)
+            done += 1
     sum_quarters(len(PIECES) - 1)
-    finish(CHUNKS - 1)
+    for chunk in range(done, CHUNKS):
+        finish(chunk)
 
     for piece, (chunk, lanes) in enumerate(PIECES):
         settle(sent(piece), amp_send.at[piece])

time: 170 us -> 168 us (0.988)
  Pallas kernels: 163 us -> 161 us
    pallas_call x1, Pallas kernels: 163 us -> 161 us  [per_device(): pl.pallas_call(kernel, out_shape=jax.ShapeDtypeStruct((COLS_OUT, BLOCK),...]
where the time goes in v4:
time: 168 us; the launch traced here: 165 us
  Pallas kernels  161 us (96%)
  local copies, waits for them, and re-layouts  3.81 us (2%)
    pallas_call x1, Pallas kernels, per_device(): pl.pallas_call(kernel, out_shape=jax.ShapeDtypeStruct((COLS_OUT, BLOCK),...  161 us

profile of v4, /device:TPU:1, one launch (start us, length us, event | category | flops | bytes accessed | tf_op | source)
XLA Modules:
  0.0 164.9 jit_solution(5723630588068922698)
XLA Ops:
  0.0 0.0 copy-start
  0.0 0.7 copy-done
  0.7 0.8 copy.6.col_energy
  1.5 161.1 %shard_map.55 = f32[256,1024]{1,0:T(8,128)} custom-call(bf16[1,44,65536]{2,1,0:T(8,128)(2,1)} %amp.1, bf16[1,2816,128]{2,1,0:T(8,128)(2,1)} %integrals.1, s32[8,2816]{1,0:T(8,128)} %allowed.1, f32[1,1024]{1,0:T(1,128)} %bitcast.3, f32[256,1]{1,0:T(8,128)} %copy.6.col_energy), custom_call_target="tpu_custom_call" | custom-call | flops 6442450944 | bytes 8388608 | tf_op jit(solution)/shard_map/pallas_call | solution.py:377
  162.6 2.3 %copy.8 = f32[256,1024]{1,0:T(8,128)} copy(f32[256,1024]{1,0:T(8,128)} %shard_map.55) | data formatting | bytes 2097152
  (1 shorter events, 0.0 us)
Async XLA Ops:
  0.0 0.7 copy-start
